TPU v7x, 1024 devices: a whole 8x8x8 slice. The times are simulated.
1024 devices in a mesh: section: 2 (over z_hi), tensor: 64 (over y, x), dp: 8 (over z_lo, core).
Axes of the slice: x: 8, y: 8, z: 8 (z_hi: 2, z_lo: 4; z = z_hi * 4 + z_lo), core: 2. Of those that a mesh axis runs over, the one named last changes fastest.
Arguments:
- tokens: bfloat16 [1024, 4096], P('dp', 'tensor'), may hold values from -6 to 6
- section_weights: bfloat16 [2, 4096, 14336], P('section', None, 'tensor'), may hold values from -0.09375 to 0.09375
- up_weight: bfloat16 [4096, 14336], P(None, 'tensor'), may hold values from -0.09375 to 0.09375
- cotangent: bfloat16 [1024, 4096], P('dp'), may hold values from -0.1796875 to 0.1796875
Outputs:
- section_grads: bfloat16 [2, 4096, 14336], P('section', 'dp', 'tensor')
- up_grads: bfloat16 [4096, 14336], P(('section', 'dp'), 'tensor')
All inputs are finite; a program needn't handle non-finite values.
Results may differ from a plain program's by a relative error of at most 0.018.
Values may be sent and summed in bfloat16 or wider, within the bound.
A program may use at most 32 MiB of HBM per device.

v0:
```python
import jax
import jax.numpy as jnp
from jax import lax
from jax.sharding import PartitionSpec as P


def joined_along(tiles, dim):
    lengths = list(tiles.shape[1:])
    lengths[dim] *= tiles.shape[0]
    return jnp.moveaxis(tiles, 0, dim).reshape(lengths)


def copy_for_each(shard, axis):
    peers = lax.axis_size(axis)
    return lax.all_to_all(
        jnp.broadcast_to(shard[None], (peers, *shard.shape)), axis, 0, 0, tiled=True
    )


def gather_directly(shard, axis, dim):
    return joined_along(copy_for_each(shard, axis), dim)


def passed_along(value, axis, steps):
    count = lax.axis_size(axis)
    first, last = (max(0, -steps), min(count, count - steps))
    return lax.ppermute(value, axis, [(source, source + steps) for source in range(first, last)])


def split_up(shard, dim, peers):
    lengths = shard.shape
    tiles = shard.reshape(*lengths[:dim], peers, lengths[dim] // peers, *lengths[dim + 1 :])
    return jnp.moveaxis(tiles, dim, 0)


def sum_packed(arrays, axis, dims):
    peers = lax.axis_size(axis)
    tiles = [split_up(a, dim, peers) for a, dim in zip(arrays, dims)]
    lines = jnp.concatenate([b.reshape(peers, -1) for b in tiles], axis=1)
    width = max(16, -(-lines.shape[1] // 1024) * 8)
    lines = jnp.pad(lines, ((0, 0), (0, width * 128 - lines.shape[1]))).reshape(-1, 128)
    vector, at, done = (lax.psum_scatter(lines, axis, tiled=True).reshape(-1), 0, [])
    for b in tiles:
        part = b[0]
        done.append(vector[at : at + part.size].reshape(part.shape))
        at += part.size
    return tuple(done)


def matmul(left, right):
    return jnp.dot(left, right, preferred_element_type=jnp.float32)


def along_rows(left, right):
    return lax.dot_general(
        left, right, (((0,), (0,)), ((), ())), preferred_element_type=jnp.float32
    )


def local(tokens, section_weights, up_weight, cotangent):
    section = lax.axis_index("section")
    is_first = section == 0
    slot = section_weights[0]
    tokens_all = gather_directly(tokens, "tensor", 1)
    count = tokens_all.shape[0]
    width = tokens_all.shape[1]
    half_width = width // 2
    units = slot.shape[1]

    def first_product():
        return matmul(tokens_all, slot)

    def second_product():
        return matmul(tokens_all, up_weight)

    product = lax.cond(is_first, first_product, second_product)
    gate_pre = passed_along(product.astype(jnp.bfloat16), "section", 1).astype(product.dtype)

    def second_backward():
        sigmoid_gate = jax.nn.sigmoid(gate_pre)
        hidden = (gate_pre * sigmoid_gate * product).astype(jnp.bfloat16)
        grad_hidden = matmul(cotangent, slot)
        grad_gate = (
            grad_hidden * product * sigmoid_gate * (1.0 + gate_pre * (1.0 - sigmoid_gate))
        ).astype(jnp.bfloat16)
        grad_up = (grad_hidden * gate_pre * sigmoid_gate).astype(jnp.bfloat16)
        return (grad_gate, grad_up, hidden)

    def first_backward():
        blank = jnp.zeros((count, units), jnp.bfloat16)
        return (blank, blank, blank)

    grad_gate, grad_up, hidden = lax.cond(is_first, first_backward, second_backward)
    back_gate, back_up = passed_along((grad_gate, grad_up), "section", -1)
    up_tokens = lax.dynamic_slice_in_dim(tokens_all, section * half_width, half_width, 1)
    grad_up_used = jnp.where(is_first, back_up, grad_up)
    up_part = along_rows(up_tokens, grad_up_used)
    left_rows = jnp.where(is_first, tokens_all, cotangent)
    right_rows = jnp.where(is_first, back_gate, hidden)
    slot_part = along_rows(left_rows, right_rows)
    slot_sum, up_sum = tuple(
        (
            part.astype(jnp.float32)
            for part in sum_packed(
                (slot_part.astype(jnp.bfloat16), up_part.astype(jnp.bfloat16)), "dp", (0, 0)
            )
        )
    )
    return (slot_sum.astype(jnp.bfloat16)[None], up_sum.astype(jnp.bfloat16))


def solution(mesh):
    placed = (P("dp", "tensor"), P("section", None, "tensor"), P(None, "tensor"), P("dp", None))
    return jax.shard_map(
        local,
        mesh=mesh,
        in_specs=placed,
        out_specs=(P("section", "dp", "tensor"), P(("section", "dp"), "tensor")),
        check_vma=False,
    )
```

profile of v0, /device:TPU:1, one launch (start us, length us, event | category | flops | bytes accessed | tf_op | source)
XLA Modules:
  0.0 162.1 jit_solution(17428611709526587346)
XLA Ops:
  7.2 1.9 %broadcast_in_dim.4 = bf16[64,128,64]{1,2,0:T(8,128)(2,1)} broadcast(bf16[128,64]{0,1:T(8,128)(2,1)} %param.8), dimensions={1,2} | broadcast | bytes 1064960 | tf_op jit(solution)/shard_map/broadcast_in_dim | solution.py:16
  9.1 14.0 %all-to-all-start = ((bf16[64,128,64]{1,2,0:T(8,128)(2,1)}), bf16[64,128,64]{1,2,0:T(8,128)(2,1)S(1)}, u32[]{:S(2)}, u32[]{:S(2)}) async-start(bf16[64,128,64]{1,2,0:T(8,128)(2,1)} %broadcast_in_dim.4), calls=%async_computation | async-start | bytes 2097152 | tf_op jit(solution)/shard_map/all_to_all | solution.py:15
  23.2 3.2 %copy.11 = bf16[1,4096,224]{2,1,0:T(8,128)(2,1)S(1)} copy(bf16[1,4096,224]{1,2,0:T(8,128)(2,1)} %param.9) | data formatting | bytes 3670016 | tf_op args[1]
  26.4 20.2 %all-to-all-done = bf16[64,128,64]{1,2,0:T(8,128)(2,1)S(1)} async-done(((bf16[64,128,64]{1,2,0:T(8,128)(2,1)}), bf16[64,128,64]{1,2,0:T(8,128)(2,1)S(1)}, u32[]{:S(2)}, u32[]{:S(2)}) %all-to-all-start) | async-done | bytes 1048608 | tf_op jit(solution)/shard_map/all_to_all | solution.py:15
  46.6 0.9 conditional.2
  46.6 0.9 fusion.9
  47.6 19.4 %collective-permute-start = (bf16[128,224]{0,1:T(8,128)(2,1)S(1)}, bf16[128,224]{0,1:T(8,128)(2,1)S(1)}, u32[]{:S(2)}, u32[]{:S(2)}) collective-permute-start(bf16[128,224]{0,1:T(8,128)(2,1)S(1)} %convert_element_type.30), channel_id=1, source_target_pairs={{0,512},{1,513},{2,514},{3,515},{4,516},{5,517},{6,518},{7,519},{8... | collective-permute-start | bytes 172040 | tf_op jit(solution)/shard_map/ppermute | solution.py:27
  67.0 1.2 collective-permute-done
  68.3 1.3 collective-permute-start.2
  69.6 1.6 copy.10
  71.3 1.5 collective-permute-start.1
  72.7 6.8 %collective-permute-done.2 = bf16[128,224]{0,1:T(8,128)(2,1)S(1)} collective-permute-done((bf16[128,224]{0,1:T(8,128)(2,1)S(1)}, bf16[128,224]{0,1:T(8,128)(2,1)S(1)}, u32[]{:S(2)}, u32[]{:S(2)}) %collective-permute-start.2) | collective-permute-done | bytes 57376 | tf_op jit(solution)/shard_map/ppermute | solution.py:27
  79.6 1.3 convolution_convert_fusion.1
  80.9 1.5 copy.16
  82.3 2.8 %reshape_reshape.7 = bf16[8,57344]{1,0:T(8,128)(2,1)} reshape(bf16[2048,224]{1,0:T(8,128)(2,1)S(1)} %copy.16) | data formatting | bytes 1835008 | tf_op jit(solution)/shard_map/reshape;reshape | solution.py:39
  85.1 1.9 %convolution_convert_fusion = bf16[4096,224]{0,1:T(8,128)(2,1)} fusion(bf16[128,4096]{0,1:T(8,128)(2,1)S(1)} %bitcast.13, bf16[128,4096]{0,1:T(8,128)(2,1)S(1)} %copy.10, pred[]{:T(512)S(6)} %eq.3, bf16[128,224]{0,1:T(8,128)(2,1)S(1)} %collective-permute-done.1, bf16[128,224]{0,1:T(8,128)(2,1)S(1)} %get-tuple-element.33), kind=kOutput, calls=%fused_computation.4 | convolution fusion | flops 236351488 | bytes 4046849 | tf_op jit(solution)/shard_map/dot_general | solution.py:55
  87.0 3.2 %copy.15 = bf16[4096,224]{1,0:T(8,128)(2,1)S(1)} copy(bf16[4096,224]{0,1:T(8,128)(2,1)} %convolution_convert_fusion) | data formatting | bytes 3670016 | tf_op jit(solution)/shard_map/convert_element_type | solution.py:105
  90.3 5.1 %reshape.24 = bf16[917504]{0:T(1024)(128)(2,1)} reshape(bf16[4096,224]{1,0:T(8,128)(2,1)S(1)} %copy.15) | data formatting | bytes 3670016
  95.4 3.5 %reshape_reshape.6 = bf16[8,114688]{1,0:T(8,128)(2,1)} reshape(bf16[917504]{0:T(1024)(128)(2,1)} %reshape.24) | data formatting | bytes 3670016 | tf_op jit(solution)/shard_map/reshape;reshape | solution.py:39
  98.9 2.9 %pad_maximum_fusion = bf16[8,172032]{1,0:T(8,128)(2,1)S(1)} fusion(bf16[8,57344]{1,0:T(8,128)(2,1)} %reshape_reshape.7, bf16[8,114688]{1,0:T(8,128)(2,1)} %reshape_reshape.6), kind=kLoop, calls=%fused_computation.5 | loop fusion | flops 5505024 | bytes 5505024 | tf_op jit(solution)/shard_map/concatenate | solution.py:39
  101.8 2.8 %reshape.22 = bf16[10752,128]{1,0:T(8,128)(2,1)} reshape(bf16[8,172032]{1,0:T(8,128)(2,1)S(1)} %pad_maximum_fusion) | data formatting | bytes 5505024 | tf_op jit(solution)/shard_map/reshape | solution.py:41
  104.6 46.7 %reduce-scatter.2.cloned.1.call-done = bf16[1344,128]{1,0:T(8,128)(2,1)} async-done(((bf16[10752,128]{1,0:T(8,128)(2,1)}), bf16[1344,128]{1,0:T(8,128)(2,1)}) %reduce-scatter.2.cloned.1.call-update) | async-done | bytes 344080 | tf_op jit(solution)/shard_map/reduce_scatter | solution.py:42
  151.3 0.9 slice.11
  153.2 1.0 slice.10
  (13 shorter events, 2.2 us)
Async XLA Ops:
  9.1 37.5 %all-to-all-start = ((bf16[64,128,64]{1,2,0:T(8,128)(2,1)}), bf16[64,128,64]{1,2,0:T(8,128)(2,1)S(1)}, u32[]{:S(2)}, u32[]{:S(2)}) async-start(bf16[64,128,64]{1,2,0:T(8,128)(2,1)} %broadcast_in_dim.4), calls=%async_computation | async-start | bytes 2097152 | tf_op jit(solution)/shard_map/all_to_all | solution.py:15
  23.1 128.2 %reduce-scatter.2.cloned.1.call-start = ((), (), s32[]{:S(2)}) async-start(), calls=%async_computation.2 | async-start | bytes 3096576 | tf_op jit(solution)/shard_map/reduce_scatter | solution.py:42
  47.6 20.7 %collective-permute-start = (bf16[128,224]{0,1:T(8,128)(2,1)S(1)}, bf16[128,224]{0,1:T(8,128)(2,1)S(1)}, u32[]{:S(2)}, u32[]{:S(2)}) collective-permute-start(bf16[128,224]{0,1:T(8,128)(2,1)S(1)} %convert_element_type.30), channel_id=1, source_target_pairs={{0,512},{1,513},{2,514},{3,515},{4,516},{5,517},{6,518},{7,519},{8... | collective-permute-start | bytes 172040 | tf_op jit(solution)/shard_map/ppermute | solution.py:27
  68.3 11.2 %collective-permute-start.2 = (bf16[128,224]{0,1:T(8,128)(2,1)S(1)}, bf16[128,224]{0,1:T(8,128)(2,1)S(1)}, u32[]{:S(2)}, u32[]{:S(2)}) collective-permute-start(bf16[128,224]{0,1:T(8,128)(2,1)S(1)} %get-tuple-element.34), channel_id=1, source_target_pairs={{512,0},{513,1},{514,2},{515,3},{516,4},{517,5},{518,6},{519,7},{5... | collective-permute-start | bytes 172040 | tf_op jit(solution)/shard_map/ppermute | solution.py:27
  71.3 13.9 %collective-permute-start.1 = (bf16[128,224]{0,1:T(8,128)(2,1)S(1)}, bf16[128,224]{0,1:T(8,128)(2,1)S(1)}, u32[]{:S(2)}, u32[]{:S(2)}) collective-permute-start(bf16[128,224]{0,1:T(8,128)(2,1)S(1)} %get-tuple-element.32), channel_id=1, source_target_pairs={{512,0},{513,1},{514,2},{515,3},{516,4},{517,5},{518,6},{519,7},{5... | collective-permute-start | bytes 172040 | tf_op jit(solution)/shard_map/ppermute | solution.py:27
Sparse Core Ops, SparseCore 0:
  104.7 46.5 reduce-scatter.1
where the time goes:
time: 164 us; the launch traced here: 162 us
  waiting for transfers between devices  75 us (46%)
  starting transfers between devices  36.3 us (22%)
  local copies, waits for them, and re-layouts  29.6 us (18%)
  between operations  14.2 us (9%)
  matrix products  4.14 us (3%)
  other arithmetic  2.9 us (2%)
    reduce_scatter x1, waiting for transfers between devices, sum_packed(): lax.psum_scatter(lines, axis, tiled=True).reshape(-1)  46.7 us
    ppermute x3, starting transfers between devices, passed_along(): lax.ppermute(value, axis, [(source, source + steps) for source in range(f...  22.2 us
    all_to_all x1, waiting for transfers between devices, copy_for_each(): lax.all_to_all(jnp.broadcast_to(shard[None], (peers, *shard.shape)), axis...  20.2 us
    all_to_all x1, starting transfers between devices, copy_for_each(): lax.all_to_all(jnp.broadcast_to(shard[None], (peers, *shard.shape)), axis...  14 us
    unnamed x5, local copies, waits for them, and re-layouts  11.5 us
    ppermute x3, waiting for transfers between devices, passed_along(): lax.ppermute(value, axis, [(source, source + steps) for source in range(f...  8.04 us
    another operation x2, local copies, waits for them, and re-layouts, sum_packed(): lines = jnp.concatenate([b.reshape(peers, -1) for b in tiles], axis=1)  6.31 us
  transfers between devices with their start and end apart: 5, of which 4 were waited for; matrix products, arithmetic and copies ran while one was open for 6% of the time, Pallas kernels for 0%

commit v1 on v0

v1 whole, which is shorter than its diff:
```python
import jax
import jax.numpy as jnp
from jax import lax
from jax.experimental import pallas as pl
from jax.experimental.pallas import tpu as pltpu
from jax.sharding import PartitionSpec as P

MESH = pl.DeviceIdType.MESH
BF, F32 = jnp.bfloat16, jnp.float32
NT = (((1,), (1,)), ((), ()))


def mod8(v):
    return lax.rem(v + 16, 8)


def kernel(
    tok, slot_w, up_w, cot,
    out_slot, out_up,
    x1, x2, units, wf, wd, cot_v, cot_t, res_slot, res_up,
    load_sem, local_sem,
    p1_send, p1_recv, ring_send, ring_recv,
    perm_send, perm_recv, scat_send,
    gh_send, gh_recv, ghs_send, ghs_recv,
    z_send, z_recv, sib_send, sib_recv,
):
    s = lax.axis_index("section")
    t = lax.axis_index("tensor")
    dp = lax.axis_index("dp")
    y, x = t // 8, lax.rem(t, 8)
    zl, core = dp // 2, lax.rem(dp, 2)
    z = s * 4 + zl
    sib = {"dp": zl * 2 + 1 - core}
    even = core == 0
    o_me = jnp.where(even, y, x)
    i_me = jnp.where(even, x, y)
    so = jnp.where(even, 8, 1)
    si = jnp.where(even, 1, 8)

    def inner_dev(i):
        return {"tensor": o_me * so + i * si}

    def outer_dev(o):
        return {"tensor": o * so + i_me * si}

    def z_dev(zz, c=core):
        return {"section": zz // 4, "dp": lax.rem(zz, 4) * 2 + c}

    def remote(src, dst, ss, rs, dev):
        return pltpu.make_async_remote_copy(
            src_ref=src, dst_ref=dst, send_sem=ss, recv_sem=rs,
            device_id=dev, device_id_type=MESH,
        )

    own1 = x1.at[o_me, i_me]
    ld_tok = pltpu.make_async_copy(tok, own1, load_sem.at[0])
    ld_tok.start()

    @pl.when(s == 0)
    def _():
        pltpu.make_async_copy(slot_w, wf, load_sem.at[1]).start()

    @pl.when(s == 1)
    def _():
        pltpu.make_async_copy(slot_w, wd, load_sem.at[2]).start()
        pltpu.make_async_copy(cot, cot_v, load_sem.at[3]).start()
        pltpu.make_async_copy(up_w, wf, load_sem.at[1]).start()

    perm_t, perm_d = dp * 8 + x, y
    has_perm = jnp.logical_and(s == 0, y != dp)
    up_src_y = s * 4 + dp // 2
    up_src_x = lax.rem(dp, 2) * 4 + x // 2
    up_src_t = up_src_y * 8 + up_src_x
    up_src_self = jnp.logical_and(up_src_t == t, y == dp)
    up_sends = y // 4 == s
    up_dst_d = lax.rem(y, 4) * 2 + x // 4
    up_dst_x = [lax.rem(x, 4) * 2 + h for h in range(2)]
    up_dst_t = [dp * 8 + v for v in up_dst_x]
    up_dst_self = [jnp.logical_and(v == t, up_dst_d == dp) for v in up_dst_t]

    barrier = pltpu.get_barrier_semaphore()

    def greet(dev):
        pl.semaphore_signal(barrier, inc=1, device_id=dev, device_id_type=MESH)

    for k in range(1, 8):
        greet(inner_dev(mod8(i_me + k)))
    greet(outer_dev(mod8(o_me + 1)))
    greet(outer_dev(mod8(o_me - 1)))
    for k in range(1, 8):
        greet(z_dev(mod8(z + k)))
        greet(z_dev(mod8(z + k), 1 - core))
    greet(sib)

    @pl.when(has_perm)
    def _():
        greet({"tensor": perm_t, "dp": perm_d})

    @pl.when(jnp.logical_not(up_src_self))
    def _():
        greet({"tensor": up_src_t, "dp": y})

    ld_tok.wait()
    expected = 7 + 2 + 15 + has_perm.astype(jnp.int32)
    for h in range(2):
        expected += jnp.logical_and(up_sends, jnp.logical_not(up_dst_self[h])).astype(jnp.int32)
    pl.semaphore_wait(barrier, expected)

    def p1_copy(buf, n, k):
        own = buf.at[o_me, i_me]
        return remote(own, own, p1_send.at[n, k - 1], p1_recv.at[n, k - 1],
                      inner_dev(mod8(i_me + k)))

    def ring_copy(buf, n, way, d, c):
        sign = 1 if way == 0 else -1
        block = mod8(o_me - sign * (d - 1))
        part = buf.at[block, pl.ds(2 * c, 2)]
        at = (d - 1) * 4 + c
        return remote(part, part, ring_send.at[n, way, at], ring_recv.at[n, way, at],
                      outer_dev(mod8(o_me + sign)))

    def ring_chunks(way, d):
        if d < 4:
            return range(4)
        return range(2) if way == 0 else range(2, 4)

    def p1_start(buf, n):
        for k in range(1, 8):
            p1_copy(buf, n, k).start()

    def p1_wait(buf, n):
        for k in range(1, 8):
            p1_copy(buf, n, k).wait_recv()

    def ring_step(buf, n, d):
        for c in range(4):
            for way in range(2):
                if c in ring_chunks(way, d):
                    if d > 1:
                        ring_copy(buf, n, way, d - 1, c).wait_recv()
                    ring_copy(buf, n, way, d, c).start()

    def ring_rest(buf, n):
        for c in range(4):
            for way in range(2):
                if c not in ring_chunks(way, 4):
                    ring_copy(buf, n, way, 3, c).wait_recv()
                else:
                    ring_copy(buf, n, way, 4, c).wait_recv()

    def all_sends(buf, n):
        for k in range(1, 8):
            p1_copy(buf, n, k).wait_send()
        for d in range(1, 5):
            for way in range(2):
                for c in ring_chunks(way, d):
                    ring_copy(buf, n, way, d, c).wait_send()

    p1_start(x1, 0)

    own2 = x2.at[o_me, i_me]

    def slot_at(d_core, yy, xx):
        return jnp.where(d_core == 0, yy, xx), jnp.where(d_core == 0, xx, yy)

    def perm_copy():
        a, b = slot_at(lax.rem(y, 2), dp, x)
        return remote(own1, x2.at[a, b, pl.ds(0, 64)], perm_send.at[0], perm_recv.at[0],
                      {"tensor": perm_t, "dp": perm_d})

    def up_copy(h):
        a, b = slot_at(lax.rem(up_dst_d, 2), dp, up_dst_x[h])
        return remote(own1.at[pl.ds(32 * h, 32)], x2.at[a, b, pl.ds(64, 32)],
                      perm_send.at[1 + h], perm_recv.at[1],
                      {"tensor": up_dst_t[h], "dp": up_dst_d})

    def perm_local():
        return pltpu.make_async_copy(own1, own2.at[pl.ds(0, 64)], local_sem.at[0])

    def up_local(h):
        return pltpu.make_async_copy(own1.at[pl.ds(32 * h, 32)], own2.at[pl.ds(64, 32)], local_sem.at[1])

    @pl.when(has_perm)
    def _():
        perm_copy().start()

    @pl.when(jnp.logical_and(s == 0, y == dp))
    def _():
        perm_local().start()

    for h in range(2):
        @pl.when(jnp.logical_and(up_sends, jnp.logical_not(up_dst_self[h])))
        def _():
            up_copy(h).start()

        @pl.when(jnp.logical_and(up_sends, up_dst_self[h]))
        def _():
            up_local(h).start()

    odd_rows = pl.ds(pl.multiple_of(lax.rem(x, 2) * 64, 64), 64)

    def scat_slot(g):
        a, b = (y, x) if g % 2 == 0 else (x, y)
        return x2.at[a, b, pl.ds(0, 64)]

    def scat_copy(g):
        return remote(cot_t.at[g, odd_rows], scat_slot(g), scat_send.at[g], perm_recv.at[0], {"dp": g})

    def scat_local(g):
        return pltpu.make_async_copy(cot_t.at[g, odd_rows], scat_slot(g), local_sem.at[0])

    is_scat = jnp.logical_and(s == 1, y == dp)

    def gh_copy(k):
        unit = units.at[2, dp]
        return remote(unit, unit, gh_send.at[k - 1], gh_recv.at[zl], z_dev(mod8(z + k)))

    def gh_sib(q):
        unit = units.at[2, q * 2 + core]
        return remote(unit, unit, ghs_send.at[q], ghs_recv.at[q], sib)

    @pl.when(s == 1)
    def _():
        pltpu.make_async_copy(slot_w, wd, load_sem.at[2]).wait()
        pltpu.make_async_copy(cot, cot_v, load_sem.at[3]).wait()

    @pl.when(is_scat)
    def _():
        for g in range(8):
            lanes = pl.ds(pl.multiple_of(g * 512 + (x // 2) * 128, 128), 128)
            cot_t[g] = cot_v[:, lanes].T
        for g in range(8):
            @pl.when(dp != g)
            def _():
                scat_copy(g).start()

            @pl.when(dp == g)
            def _():
                scat_local(g).start()

    @pl.when(s == 1)
    def _():
        gh = lax.dot_general(wd[...], cot_v[...], NT, preferred_element_type=F32)
        units[2, dp] = gh.astype(BF)
        for k in range(1, 8):
            gh_copy(k).start()

    p1_wait(x1, 0)
    ring_step(x1, 0, 1)

    @pl.when(jnp.logical_or(has_perm, jnp.logical_and(s == 1, y != dp)))
    def _():
        perm_copy().wait_recv()

    @pl.when(y == dp)
    def _():
        perm_local().wait()

    @pl.when(jnp.logical_not(up_src_self))
    def _():
        up_copy(0).wait_recv()

    @pl.when(up_src_self)
    def _():
        up_local(0).wait()

    ring_step(x1, 0, 2)
    p1_start(x2, 1)
    ring_step(x1, 0, 3)
    ring_step(x1, 0, 4)

    for q in range(4):
        @pl.when(jnp.logical_or(s == 0, zl != q))
        def _():
            unit = units.at[2, q * 2 + core]
            remote(unit, unit, gh_send.at[0], gh_recv.at[q], sib).wait_recv()
        gh_sib(q).start()

    p1_wait(x2, 1)
    ring_step(x2, 1, 1)
    ring_rest(x1, 0)

    @pl.when(s == 0)
    def _():
        pltpu.make_async_copy(slot_w, wf, load_sem.at[1]).wait()

    @pl.when(s == 1)
    def _():
        pltpu.make_async_copy(up_w, wf, load_sem.at[1]).wait()

    def piece1(yy, xx):
        a, b = slot_at(core, yy, xx)
        return x1[a, b]

    pre = jnp.zeros((224, 128), F32)
    for yy in range(8):
        rows = jnp.concatenate([piece1(yy, xx) for xx in range(8)], axis=0)
        pre += jnp.dot(wf[:, yy * 512 : yy * 512 + 512], rows, preferred_element_type=F32)
    units[s, dp] = pre.astype(BF)

    def z_unit(zz):
        return units.at[zz // 4, lax.rem(zz, 4) * 2 + core]

    def z_copy(way, d, c):
        sign = 1 if way == 0 else -1
        part = z_unit(mod8(z - sign * (d - 1))).at[pl.ds(112 * c, 112)]
        at = (d - 1) * 2 + c
        return remote(part, part, z_send.at[way, at], z_recv.at[way, at], z_dev(mod8(z + sign)))

    def z_chunks(way, d):
        if d < 4:
            return range(2)
        return range(1) if way == 0 else range(1, 2)

    def z_sib(k):
        unit = z_unit(mod8(z + k))
        return remote(unit, unit, sib_send.at[k], sib_recv.at[k], sib)

    def z_step(d):
        for c in range(2):
            for way in range(2):
                if d > 1:
                    z_copy(way, d - 1, c).wait_recv()
                if c in z_chunks(way, d):
                    z_copy(way, d, c).start()

    z_step(1)
    z_sib(0).start()
    ring_step(x2, 1, 2)
    z_step(2)
    z_sib(7).start()
    z_sib(1).start()
    ring_step(x2, 1, 3)
    z_step(3)
    z_sib(6).start()
    z_sib(2).start()
    ring_step(x2, 1, 4)
    z_step(4)
    z_sib(5).start()
    z_sib(3).start()
    z_copy(0, 4, 0).wait_recv()
    z_copy(1, 4, 1).wait_recv()
    z_sib(4).start()

    for q in range(4):
        gh_sib(q).wait_recv()
    for k in range(8):
        z_sib(k).wait_recv()
    ring_rest(x2, 1)

    total_slot = jnp.zeros((224, 512), F32)
    total_up = jnp.zeros((224, 256), F32)

    def piece2(g, xx):
        a, b = slot_at(core, g, xx)
        return x2[a, b]

    is_first = s == 0
    for pair in range(4):
        lefts, ups, rows_slot, rows_up = [], [], [], []
        for g in (2 * pair, 2 * pair + 1):
            gate = units[0, g].astype(F32)
            up = units[1, g].astype(F32)
            gh = units[2, g].astype(F32)
            sg = jax.nn.sigmoid(gate)
            act = gate * sg
            lefts.append(jnp.where(
                is_first, gh * up * sg * (1.0 + gate * (1.0 - sg)), act * up).astype(BF))
            ups.append((gh * act).astype(BF))
            pieces = [piece2(g, xx) for xx in range(8)]
            rows_slot.append(jnp.concatenate([v[:64] for v in pieces], axis=0))
            rows_up.append(jnp.concatenate([v[64:] for v in pieces], axis=0))
        total_slot += lax.dot_general(
            jnp.concatenate(lefts, axis=1), jnp.concatenate(rows_slot, axis=1), NT,
            preferred_element_type=F32)
        total_up += lax.dot_general(
            jnp.concatenate(ups, axis=1), jnp.concatenate(rows_up, axis=1), NT,
            preferred_element_type=F32)
    res_slot[...] = total_slot.astype(BF)
    res_up[...] = total_up.astype(BF)
    st_slot = pltpu.make_async_copy(res_slot, out_slot, load_sem.at[0])
    st_up = pltpu.make_async_copy(res_up, out_up, load_sem.at[1])
    st_slot.start()
    st_up.start()

    all_sends(x1, 0)
    all_sends(x2, 1)

    @pl.when(has_perm)
    def _():
        perm_copy().wait_send()

    for h in range(2):
        @pl.when(jnp.logical_and(up_sends, jnp.logical_not(up_dst_self[h])))
        def _():
            up_copy(h).wait_send()

    @pl.when(is_scat)
    def _():
        for g in range(8):
            @pl.when(dp != g)
            def _():
                scat_copy(g).wait_send()

    @pl.when(s == 1)
    def _():
        for k in range(1, 8):
            gh_copy(k).wait_send()

    for q in range(4):
        gh_sib(q).wait_send()
    for k in range(8):
        z_sib(k).wait_send()
    for way in range(2):
        for d in range(1, 5):
            for c in z_chunks(way, d):
                z_copy(way, d, c).wait_send()
    st_slot.wait()
    st_up.wait()


def local(tokens, section_weights, up_weight, cotangent):
    dma = pltpu.SemaphoreType.DMA
    any_spec = pl.BlockSpec(memory_space=pl.ANY)
    slot_t, up_t = pl.pallas_call(
        kernel,
        out_shape=(jax.ShapeDtypeStruct((224, 512), BF), jax.ShapeDtypeStruct((224, 256), BF)),
        in_specs=[any_spec] * 4,
        out_specs=(any_spec, any_spec),
        scratch_shapes=[
            pltpu.VMEM((8, 8, 64, 128), BF),
            pltpu.VMEM((8, 8, 96, 128), BF),
            pltpu.VMEM((3, 8, 224, 128), BF),
            pltpu.VMEM((224, 4096), BF),
            pltpu.VMEM((224, 4096), BF),
            pltpu.VMEM((128, 4096), BF),
            pltpu.VMEM((8, 128, 128), BF),
            pltpu.VMEM((224, 512), BF),
            pltpu.VMEM((224, 256), BF),
            dma((4,)), dma((2,)),
            dma((2, 7)), dma((2, 7)), dma((2, 2, 16)), dma((2, 2, 16)),
            dma((3,)), dma((2,)), dma((8,)),
            dma((7,)), dma((4,)), dma((4,)), dma((4,)),
            dma((2, 8)), dma((2, 8)), dma((8,)), dma((8,)),
        ],
        compiler_params=pltpu.CompilerParams(
            collective_id=0, has_side_effects=True, vmem_limit_bytes=40 * 1024 * 1024
        ),
        cost_estimate=pl.CostEstimate(flops=10**9, bytes_accessed=10**7, transcendentals=10**6),
    )(tokens.T, section_weights[0].T, up_weight.T, cotangent)
    return slot_t.T[None], up_t.T


def solution(mesh):
    placed = (P("dp", "tensor"), P("section", None, "tensor"), P(None, "tensor"), P("dp", None))
    return jax.shard_map(
        local,
        mesh=mesh,
        in_specs=placed,
        out_specs=(P("section", "dp", "tensor"), P(("section", "dp"), "tensor")),
        check_vma=False,
    )
```

time: 164 us -> 71 us (0.43); the launches traced: 162 us -> 70.7 us
  waiting for transfers between devices: 75 us -> 0 us
  Pallas kernels: 0 us -> 63.8 us
  starting transfers between devices: 36.3 us -> 0 us
  local copies, waits for them, and re-layouts: 29.6 us -> 6.27 us
  between operations: 14.2 us -> 0.65 us
  matrix products: 4.14 us -> 0 us
  other arithmetic: 2.9 us -> 0 us
    pallas_call x0 -> x1, Pallas kernels: none -> 63.8 us  [local(): pl.pallas_call(kernel, out_shape=(jax.ShapeDtypeStruct((224, 512), BF), j...]
    reduce_scatter x1 -> x0, waiting for transfers between devices: 46.7 us -> none  [sum_packed(): lax.psum_scatter(lines, axis, tiled=True).reshape(-1)]
    ppermute x3 -> x0, starting transfers between devices: 22.2 us -> none  [passed_along(): lax.ppermute(value, axis, [(source, source + steps) for source in range(f...]
    all_to_all x1 -> x0, waiting for transfers between devices: 20.2 us -> none  [copy_for_each(): lax.all_to_all(jnp.broadcast_to(shard[None], (peers, *shard.shape)), axis...]
    all_to_all x1 -> x0, starting transfers between devices: 14 us -> none  [copy_for_each(): lax.all_to_all(jnp.broadcast_to(shard[None], (peers, *shard.shape)), axis...]
    ppermute x3 -> x0, waiting for transfers between devices: 8.04 us -> none  [passed_along(): lax.ppermute(value, axis, [(source, source + steps) for source in range(f...]
    another operation x5 -> x0, local copies, waits for them, and re-layouts: 6.34 us -> none  [the longest x2 6.31 us: sum_packed(): lines = jnp.concatenate([b.reshape(peers, -1) for b in tiles], axis=1)]
    unnamed x5 -> x10, local copies, waits for them, and re-layouts: 11.5 us -> 6.27 us
  transfers between devices with their start and end apart: 5 -> 0, of which waited for: 4 -> 0; matrix products, arithmetic and copies ran while one was open for 6% -> 0% of each run, Pallas kernels for 0% -> 0%
where the time goes in v1:
time: 71 us; the launch traced here: 70.7 us
  Pallas kernels  63.8 us (90%)
  local copies, waits for them, and re-layouts  6.27 us (9%)
    pallas_call x1, Pallas kernels, local(): pl.pallas_call(kernel, out_shape=(jax.ShapeDtypeStruct((224, 512), BF), j...  63.8 us
    unnamed x10, local copies, waits for them, and re-layouts  6.27 us

profile of v1, /device:TPU:1, one launch (start us, length us, event | category | flops | bytes accessed | tf_op | source)
XLA Modules:
  0.0 70.7 jit_solution(13762090488490395221)
XLA Ops:
  0.6 0.0 copy-start
  0.6 1.5 %copy-done = bf16[1,4096,224]{1,2,0:T(8,128)(2,1)S(1)} copy-done((bf16[1,4096,224]{1,2,0:T(8,128)(2,1)S(1)}, bf16[1,4096,224]{1,2,0:T(8,128)(2,1)}, u32[]{:S(2)}) %copy-start) | copy-done | bytes 1835032
  2.1 0.0 copy-start.1
  2.1 1.5 %copy-done.1 = bf16[4096,224]{0,1:T(8,128)(2,1)S(1)} copy-done((bf16[4096,224]{0,1:T(8,128)(2,1)S(1)}, bf16[4096,224]{0,1:T(8,128)(2,1)}, u32[]{:S(2)}) %copy-start.1) | copy-done | bytes 1835032
  3.6 0.0 copy-start.2
  3.6 1.2 %copy-done.2 = bf16[128,4096]{1,0:T(8,128)(2,1)S(1)} copy-done((bf16[128,4096]{1,0:T(8,128)(2,1)S(1)}, bf16[128,4096]{1,0:T(8,128)(2,1)}, u32[]{:S(2)}) %copy-start.2) | copy-done | bytes 1048600
  4.9 0.0 copy-start.3
  4.9 0.7 %copy-done.3 = bf16[128,64]{0,1:T(8,128)(2,1)S(1)} copy-done((bf16[128,64]{0,1:T(8,128)(2,1)S(1)}, bf16[128,64]{0,1:T(8,128)(2,1)}, u32[]{:S(2)}) %copy-start.3) | copy-done | bytes 16408
  5.6 63.8 %shard_map.59 = (bf16[224,512]{1,0:T(8,128)(2,1)S(1)}, bf16[224,256]{1,0:T(8,128)(2,1)S(1)}) custom-call(bf16[64,128]{1,0:T(8,128)(2,1)S(1)} %bitcast.13, bf16[224,4096]{1,0:T(8,128)(2,1)S(1)} %bitcast.9, bf16[224,4096]{1,0:T(8,128)(2,1)S(1)} %bitcast.10, bf16[128,4096]{1,0:T(8,128)(2,1)S(1)} %copy-done.2), custom_call_target="tpu_custom_call" | custom-call | flops 1000000000 | bytes 10000000 | tf_op jit(solution)/shard_map/pallas_call | solution.py:425
  69.4 0.7 copy.8
  70.1 0.6 copy.9
Async XLA Ops:
  0.6 1.5 %copy-start = (bf16[1,4096,224]{1,2,0:T(8,128)(2,1)S(1)}, bf16[1,4096,224]{1,2,0:T(8,128)(2,1)}, u32[]{:S(2)}) copy-start(bf16[1,4096,224]{1,2,0:T(8,128)(2,1)} %param.5) | copy-start | bytes 5505028
  2.1 1.5 %copy-start.1 = (bf16[4096,224]{0,1:T(8,128)(2,1)S(1)}, bf16[4096,224]{0,1:T(8,128)(2,1)}, u32[]{:S(2)}) copy-start(bf16[4096,224]{0,1:T(8,128)(2,1)} %param.6) | copy-start | bytes 5505028
  3.6 1.2 %copy-start.2 = (bf16[128,4096]{1,0:T(8,128)(2,1)S(1)}, bf16[128,4096]{1,0:T(8,128)(2,1)}, u32[]{:S(2)}) copy-start(bf16[128,4096]{1,0:T(8,128)(2,1)} %cot.1) | copy-start | bytes 3145732
  4.9 0.7 %copy-start.3 = (bf16[128,64]{0,1:T(8,128)(2,1)S(1)}, bf16[128,64]{0,1:T(8,128)(2,1)}, u32[]{:S(2)}) copy-start(bf16[128,64]{0,1:T(8,128)(2,1)} %param.4) | copy-start | bytes 49156

commit v2 on v0

v2 whole, which is shorter than its diff:
```python
import jax
import jax.numpy as jnp
from jax import lax
from jax.experimental import pallas as pl
from jax.experimental.pallas import tpu as pltpu
from jax.sharding import PartitionSpec as P

MESH = pl.DeviceIdType.MESH
BF, F32, I32 = jnp.bfloat16, jnp.float32, jnp.int32
NT = (((1,), (1,)), ((), ()))


def mod8(v):
    return lax.rem(v + 16, 8)


def both(*conditions):
    out = conditions[0]
    for c in conditions[1:]:
        out = jnp.logical_and(out, c)
    return out


def kernel(
    tok, slot_w, up_w, cot,
    out_slot, out_up,
    x1, x2, x3, units, gh_v, wf, wd, cot_v, cot_t, res_slot, res_up,
    load_sem, local_sem, ready0, ready1,
    p1_send, p1_recv, ring_send, ring_recv,
    perm_send, perm_recv, scat_send, scat_recv,
    gh_send, gh_recv,
    z_send, z_recv, sib_send, sib_recv,
):
    s = lax.axis_index("section")
    t = lax.axis_index("tensor")
    dp = lax.axis_index("dp")
    y, x = t // 8, lax.rem(t, 8)
    zl, core = dp // 2, lax.rem(dp, 2)
    z = s * 4 + zl
    first, second = s == 0, s == 1
    sib = {"dp": zl * 2 + 1 - core}
    even = core == 0
    o_me = jnp.where(even, y, x)
    i_me = jnp.where(even, x, y)
    so = jnp.where(even, 8, 1)
    si = jnp.where(even, 1, 8)

    def when(*conditions):
        return pl.when(both(*conditions))

    def count(*conditions):
        return both(*conditions).astype(I32)

    def inner_dev(i):
        return {"tensor": o_me * so + i * si}

    def outer_dev(o):
        return {"tensor": o * so + i_me * si}

    def z_dev(zz, c=core):
        return {"section": zz // 4, "dp": lax.rem(zz, 4) * 2 + c}

    def remote(src, dst, ss, rs, dev):
        return pltpu.make_async_remote_copy(
            src_ref=src, dst_ref=dst, send_sem=ss, recv_sem=rs,
            device_id=dev, device_id_type=MESH,
        )

    def slot_at(d_core, yy, xx):
        return jnp.where(d_core == 0, yy, xx), jnp.where(d_core == 0, xx, yy)

    own1, own2, own3 = x1.at[o_me, i_me], x2.at[o_me, i_me], x3.at[o_me, i_me]
    ld_tok = pltpu.make_async_copy(tok, own1, load_sem.at[0])
    ld_tok.start()

    @when(first)
    def _():
        pltpu.make_async_copy(slot_w, wf, load_sem.at[1]).start()
        pltpu.make_async_copy(up_w, wd, load_sem.at[2]).start()

    @when(second)
    def _():
        pltpu.make_async_copy(cot, cot_v, load_sem.at[3]).start()
        pltpu.make_async_copy(slot_w, wd, load_sem.at[2]).start()

    perm_t, perm_d = dp * 8 + x, y
    perm_z = y // 2
    has_perm = both(first, y != dp)
    up_src_t = (s * 4 + dp // 2) * 8 + lax.rem(dp, 2) * 4 + x // 2
    up_src_z = y // 2
    up_recvs = jnp.logical_not(both(up_src_t == t, y == dp))
    up_dst_d = lax.rem(y, 4) * 2 + x // 4
    up_dst_z = up_dst_d // 2
    up_dst_x = [lax.rem(x, 4) * 2 + h for h in range(2)]
    up_dst_t = [dp * 8 + v for v in up_dst_x]
    up_from = y // 4 == s
    up_self = [both(up_from, v == t, up_dst_d == dp) for v in up_dst_t]
    up_sends = [both(up_from, jnp.logical_not(v)) for v in up_self]

    barrier = pltpu.get_barrier_semaphore()

    def tell(sem, dev):
        pl.semaphore_signal(sem, inc=1, device_id=dev, device_id_type=MESH)

    def wait_for(sem, number):
        @when(number > 0)
        def _():
            pl.semaphore_wait(sem, number)

    def answer(dev):
        @when(first)
        def _():
            tell(ready0, dev)

        @when(second)
        def _():
            tell(ready1, dev)

    for k in range(1, 8):
        tell(barrier, inner_dev(mod8(i_me + k)))
    for k in (1, -1, 2, -2):
        tell(barrier, outer_dev(mod8(o_me + k)))
    tell(barrier, sib)

    @when(first)
    def _():
        tell(barrier, {"section": 1})

    @when(first, jnp.logical_or(zl == 0, zl == 3))
    def _():
        tell(barrier, {"section": 1, "dp": (3 - zl) * 2 + core})

    @when(first, zl < 3)
    def _():
        tell(barrier, {"dp": dp + 2})

    for q in range(1, 4):
        @when(second, zl < q)
        def _():
            tell(barrier, {"dp": 2 * q})
            tell(barrier, {"dp": 2 * q + 1})

    @when(has_perm, perm_z >= zl)
    def _():
        tell(barrier, {"tensor": perm_t, "dp": perm_d})

    @when(up_recvs, up_src_z >= zl)
    def _():
        tell(barrier, {"tensor": up_src_t, "dp": y})

    for h in range(2):
        @when(up_sends[h], up_dst_z > zl)
        def _():
            tell(barrier, {"tensor": up_dst_t[h], "dp": up_dst_d})

    expected = 12 + count(first, zl > 0) + jnp.where(second, 1 + 2 * zl, 0)
    expected += count(second, jnp.logical_or(zl == 0, zl == 3))
    expected += count(has_perm, perm_z <= zl) + count(up_recvs, up_src_z < zl)
    for h in range(2):
        expected += count(up_sends[h], up_dst_z <= zl)

    half = pl.ds(pl.multiple_of(lax.rem(y, 2) * 64, 64), 64), pl.ds(pl.multiple_of(lax.rem(x, 2) * 64, 64), 64)

    @when(second)
    def _():
        pltpu.make_async_copy(cot, cot_v, load_sem.at[3]).wait()
        for g in range(8):
            pos = y if g % 2 == 0 else x
            lanes = pl.ds(pl.multiple_of(g * 512 + (pos // 2) * 128, 128), 128)
            cot_t[g] = cot_v[:, lanes].T
        pltpu.make_async_copy(slot_w, wd, load_sem.at[2]).wait()
        gh = lax.dot_general(wd[...], cot_v[...], NT, preferred_element_type=F32)
        gh_v[...] = gh.astype(BF)

    ld_tok.wait()
    pl.semaphore_wait(barrier, expected)

    @when(first, zl > 0)
    def _():
        tell(ready0, {"dp": dp - 2})

    for q in range(3):
        @when(second, zl > q)
        def _():
            tell(ready1, {"dp": 2 * q})
            tell(ready1, {"dp": 2 * q + 1})

    @when(second, jnp.logical_or(zl == 0, zl == 3))
    def _():
        tell(ready1, {"section": 0, "dp": (3 - zl) * 2 + core})

    @when(has_perm, perm_z < zl)
    def _():
        tell(ready0, {"tensor": perm_t, "dp": perm_d})

    @when(up_recvs, up_src_z < zl)
    def _():
        answer({"tensor": up_src_t, "dp": y})

    ups_above = count(up_sends[0], up_dst_z > zl) + count(up_sends[1], up_dst_z > zl)

    def p1_copy(buf, n, k):
        own = buf.at[o_me, i_me]
        return remote(own, own, p1_send.at[n, k - 1], p1_recv.at[n, k - 1],
                      inner_dev(mod8(i_me + k)))

    def ring_copy(buf, n, way, at):
        sign = 1 if way == 0 else -1
        part = buf.at[mod8(o_me - (0 if at < 2 else 2 * sign))]
        if at == 3:
            part = part.at[pl.ds(4 * way, 4)]
        return remote(part, part, ring_send.at[n, way, at], ring_recv.at[n, way, at],
                      outer_dev(mod8(o_me + sign * (1 + at % 2))))

    def p1_start(buf, n):
        for k in range(1, 8):
            p1_copy(buf, n, k).start()

    def p1_wait(buf, n):
        for k in range(1, 8):
            p1_copy(buf, n, k).wait_recv()

    def ring_first(buf, n):
        for at in (1, 0):
            for way in range(2):
                ring_copy(buf, n, way, at).start()

    def ring_second(buf, n):
        for way in range(2):
            ring_copy(buf, n, way, 1).wait_recv()
            ring_copy(buf, n, way, 3).start()
            ring_copy(buf, n, way, 2).start()

    def ring_rest(buf, n):
        for at in (0, 2, 3):
            for way in range(2):
                ring_copy(buf, n, way, at).wait_recv()

    def p1_sent(buf, n):
        for k in range(1, 8):
            p1_copy(buf, n, k).wait_send()

    def ring_sent(buf, n):
        for at in range(4):
            for way in range(2):
                ring_copy(buf, n, way, at).wait_send()

    def perm_copy():
        a, b = slot_at(lax.rem(y, 2), dp, x)
        return remote(own1, x2.at[a, b], perm_send.at[0], perm_recv.at[0],
                      {"tensor": perm_t, "dp": perm_d})

    def up_copy(h):
        a, b = slot_at(lax.rem(up_dst_d, 2), dp, up_dst_x[h])
        return remote(own1.at[pl.ds(32 * h, 32)], x3.at[a, b],
                      perm_send.at[1 + h], perm_recv.at[1],
                      {"tensor": up_dst_t[h], "dp": up_dst_d})

    def perm_local():
        return pltpu.make_async_copy(own1, own2, local_sem.at[0])

    def up_local(h):
        return pltpu.make_async_copy(own1.at[pl.ds(32 * h, 32)], own3, local_sem.at[1])

    def up_start():
        for h in range(2):
            @when(up_sends[h])
            def _():
                up_copy(h).start()

            @when(up_self[h])
            def _():
                up_local(h).start()

    def up_wait():
        @when(up_recvs)
        def _():
            up_copy(0).wait_recv()

        @when(jnp.logical_not(up_recvs))
        def _():
            up_local(0).wait()

    def scat_copy(g):
        place = x2.at[y if g % 2 == 0 else x, dp]
        return remote(cot_t.at[g, half[g % 2]], place, scat_send.at[g], scat_recv.at[dp], {"dp": g})

    def scat_local(g):
        place = x2.at[y if g % 2 == 0 else x, dp]
        return pltpu.make_async_copy(cot_t.at[g, half[g % 2]], place, local_sem.at[0])

    def scat_arrived(g):
        place = x2.at[o_me, g]
        return remote(place, place, scat_send.at[g], scat_recv.at[g], sib)

    def gh_copy():
        return remote(gh_v, gh_v, gh_send, gh_recv, {"section": 0})

    def z_rides(way, d, c, to):
        if way == 0:
            src = to - d
            ok = both(src >= 0, src < 4, jnp.logical_or(to < 4, src >= 2))
            on = src >= 2
        else:
            src = mod8(to + d)
            ok = both(src < 4, jnp.where(to < 4, src > to, src < 2))
            on = src < 2
        return both(ok, to < 4) if c == 0 else ok if c == 1 else both(ok, on)

    def z_copy(way, d, c):
        sign = 1 if way == 0 else -1
        src = mod8(z - sign * (d - 1))
        part = units.at[lax.rem(src, 4) * 2 + core, c]
        return remote(part, part, z_send.at[way, d - 1, c], z_recv.at[way, d - 1, c], z_dev(mod8(z + sign)))

    def z_sends(way, d, c):
        return z_rides(way, d, c, mod8(z + (1 if way == 0 else -1)))

    def z_sib(k, c):
        q = lax.rem(mod8(z + k), 4)
        unit = units.at[q * 2 + core, c]
        return remote(unit, unit, sib_send.at[q, c], sib_recv.at[q, c], sib)

    def z_wanted(c):
        return first if c == 0 else second if c == 2 else jnp.logical_or(first, second)

    def z_step(d):
        for c in (1, 0, 2):
            for way in range(2):
                if d > 1:
                    @when(z_rides(way, d - 1, c, z))
                    def _():
                        z_copy(way, d - 1, c).wait_recv()

                if d < 6:
                    @when(z_sends(way, d, c))
                    def _():
                        z_copy(way, d, c).start()

                if d > 1:
                    @when(z_rides(way, d - 1, c, z), z_wanted(c))
                    def _():
                        z_sib(1 - d if way == 0 else d - 1, c).start()

    @when(first)
    def _():
        p1_start(x1, 0)
        p1_wait(x1, 0)
        ring_first(x1, 0)
        wait_for(ready0, count(zl < 3) + count(has_perm, perm_z > zl) + ups_above)

        @when(has_perm)
        def _():
            perm_copy().start()

        @when(y == dp)
        def _():
            perm_local().start()

        up_start()
        ring_second(x1, 0)

        @when(has_perm)
        def _():
            perm_copy().wait_recv()

        @when(y == dp)
        def _():
            perm_local().wait()

        up_wait()
        p1_start(x2, 1)
        p1_start(x3, 2)
        ring_rest(x1, 0)
        pltpu.make_async_copy(slot_w, wf, load_sem.at[1]).wait()
        pltpu.make_async_copy(up_w, wd, load_sem.at[2]).wait()

        gate_pre = jnp.zeros((224, 128), F32)
        up_pre = jnp.zeros((224, 128), F32)
        for yy in range(8):
            places = [slot_at(core, yy, xx) for xx in range(8)]
            rows = jnp.concatenate([x1[a, b] for a, b in places], axis=0)
            gate_pre += jnp.dot(wf[:, yy * 512 : yy * 512 + 512], rows, preferred_element_type=F32)
            up_pre += jnp.dot(wd[:, yy * 512 : yy * 512 + 512], rows, preferred_element_type=F32)
        gh_copy().wait_recv()
        grad_hidden = gh_v[...].astype(F32)
        sg = jax.nn.sigmoid(gate_pre)
        act = gate_pre * sg
        units[dp, 1] = (grad_hidden * act).astype(BF)
        units[dp, 0] = (grad_hidden * up_pre * sg * (1.0 + gate_pre * (1.0 - sg))).astype(BF)
        units[dp, 2] = (act * up_pre).astype(BF)

        @when(jnp.logical_or(zl == 0, zl == 3))
        def _():
            pl.semaphore_wait(ready1, 1)

        z_step(1)
        z_sib(0, 1).start()
        z_sib(0, 0).start()
        p1_wait(x2, 1)
        ring_first(x2, 1)
        p1_wait(x3, 2)
        ring_first(x3, 2)
        z_step(2)
        ring_second(x2, 1)
        ring_second(x3, 2)
        z_step(3)
        z_step(4)

    @when(second)
    def _():
        gh_copy().start()
        wait_for(ready1, 2 * (3 - zl) + ups_above)
        up_start()
        for g in range(8):
            @when(dp != g)
            def _():
                scat_copy(g).start()

            @when(dp == g)
            def _():
                scat_local(g).start()
        up_wait()
        p1_start(x3, 2)
        for g in range(8):
            @when(dp != g)
            def _():
                scat_arrived(g).wait_recv()

            @when(dp == g)
            def _():
                scat_local(g).wait()
        ring_first(x2, 1)
        p1_wait(x3, 2)
        ring_first(x3, 2)
        ring_second(x2, 1)
        ring_second(x3, 2)
        for d in range(2, 7):
            z_step(d)

    ring_rest(x2, 1)
    ring_rest(x3, 2)
    side = jnp.where(first, 0, 2)
    for q in range(4):
        for c in (1, side):
            unit = units.at[q * 2 + 1 - core, c]
            remote(unit, unit, sib_send.at[q, c], sib_recv.at[q, c], sib).wait_recv()

    total_slot = jnp.zeros((224, 512), F32)
    total_up = jnp.zeros((224, 256), F32)
    by_group = both(first, even)
    for pair in range(4):
        lefts, ups, rows_slot, rows_up = [], [], [], []
        for g in (2 * pair, 2 * pair + 1):
            lefts.append(units[g, side])
            ups.append(units[g, 1])
            rows_slot.append(jnp.concatenate(
                [x2[jnp.where(by_group, g, j), jnp.where(by_group, j, g)] for j in range(8)], axis=0))
            places = [slot_at(core, g, xx) for xx in range(8)]
            rows_up.append(jnp.concatenate([x3[a, b] for a, b in places], axis=0))
        total_slot += lax.dot_general(
            jnp.concatenate(lefts, axis=1), jnp.concatenate(rows_slot, axis=1), NT,
            preferred_element_type=F32)
        total_up += lax.dot_general(
            jnp.concatenate(ups, axis=1), jnp.concatenate(rows_up, axis=1), NT,
            preferred_element_type=F32)
    res_slot[...] = total_slot.astype(BF)
    res_up[...] = total_up.astype(BF)
    st_slot = pltpu.make_async_copy(res_slot, out_slot, load_sem.at[0])
    st_up = pltpu.make_async_copy(res_up, out_up, load_sem.at[1])
    st_slot.start()
    st_up.start()

    @when(first)
    def _():
        p1_sent(x1, 0)
        ring_sent(x1, 0)
        p1_sent(x2, 1)

        @when(has_perm)
        def _():
            perm_copy().wait_send()

    @when(second)
    def _():
        for g in range(8):
            @when(dp != g)
            def _():
                scat_copy(g).wait_send()
        gh_copy().wait_send()

    ring_sent(x2, 1)
    p1_sent(x3, 2)
    ring_sent(x3, 2)
    for h in range(2):
        @when(up_sends[h])
        def _():
            up_copy(h).wait_send()
    for q in range(4):
        for c in (1, side):
            unit = units.at[q * 2 + core, c]
            remote(unit, unit, sib_send.at[q, c], sib_recv.at[q, c], sib).wait_send()
    for way in range(2):
        for d in range(1, 6):
            for c in range(3):
                @when(z_sends(way, d, c))
                def _():
                    z_copy(way, d, c).wait_send()
    st_slot.wait()
    st_up.wait()


def local(tokens, section_weights, up_weight, cotangent):
    dma = pltpu.SemaphoreType.DMA
    any_spec = pl.BlockSpec(memory_space=pl.ANY)
    slot_t, up_t = pl.pallas_call(
        kernel,
        out_shape=(jax.ShapeDtypeStruct((224, 512), BF), jax.ShapeDtypeStruct((224, 256), BF)),
        in_specs=[any_spec] * 4,
        out_specs=(any_spec, any_spec),
        scratch_shapes=[
            pltpu.VMEM((8, 8, 64, 128), BF),
            pltpu.VMEM((8, 8, 64, 128), BF),
            pltpu.VMEM((8, 8, 32, 128), BF),
            pltpu.VMEM((8, 3, 224, 128), BF),
            pltpu.VMEM((224, 128), BF),
            pltpu.VMEM((224, 4096), BF),
            pltpu.VMEM((224, 4096), BF),
            pltpu.VMEM((128, 4096), BF),
            pltpu.VMEM((8, 128, 128), BF),
            pltpu.VMEM((224, 512), BF),
            pltpu.VMEM((224, 256), BF),
            dma((4,)), dma((2,)), pltpu.SemaphoreType.REGULAR, pltpu.SemaphoreType.REGULAR,
            dma((3, 7)), dma((3, 7)), dma((3, 2, 4)), dma((3, 2, 4)),
            dma((3,)), dma((2,)), dma((8,)), dma((8,)),
            dma, dma,
            dma((2, 5, 3)), dma((2, 5, 3)), dma((4, 3)), dma((4, 3)),
        ],
        compiler_params=pltpu.CompilerParams(
            collective_id=0, has_side_effects=True, vmem_limit_bytes=60 * 1024 * 1024
        ),
        cost_estimate=pl.CostEstimate(flops=10**9, bytes_accessed=10**7, transcendentals=10**6),
    )(tokens.T, section_weights[0].T, up_weight.T, cotangent)
    return slot_t.T[None], up_t.T


def solution(mesh):
    placed = (P("dp", "tensor"), P("section", None, "tensor"), P(None, "tensor"), P("dp", None))
    return jax.shard_map(
        local,
        mesh=mesh,
        in_specs=placed,
        out_specs=(P("section", "dp", "tensor"), P(("section", "dp"), "tensor")),
        check_vma=False,
    )
```

time: 164 us -> 59.6 us (0.36)
  the two profiles are of different devices: /device:TPU:1 before, /device:TPU:17 now
where the time goes in v2:
time: 59.6 us; the launch traced here: 59.4 us
  Pallas kernels  55.6 us (93%)
  local copies, waits for them, and re-layouts  3.19 us (5%)
  between operations  0.64 us (1%)
    pallas_call x1, Pallas kernels, local(): pl.pallas_call(kernel, out_shape=(jax.ShapeDtypeStruct((224, 512), BF), j...  55.6 us
    unnamed x2, local copies, waits for them, and re-layouts  3.19 us

profile of v2, /device:TPU:17, one launch (start us, length us, event | category | flops | bytes accessed | tf_op | source)
XLA Modules:
  0.0 59.4 jit_solution(2544732705396195962)
XLA Ops:
  0.6 55.6 %shard_map.59 = (bf16[224,512]{1,0:T(8,128)(2,1)}, bf16[224,256]{1,0:T(8,128)(2,1)}) custom-call(bf16[64,128]{1,0:T(8,128)(2,1)} %bitcast.13, bf16[224,4096]{1,0:T(8,128)(2,1)} %bitcast.9, bf16[224,4096]{1,0:T(8,128)(2,1)} %bitcast.10, bf16[128,4096]{1,0:T(8,128)(2,1)} %cot.1), custom_call_target="tpu_custom_call" | custom-call | flops 1000000000 | bytes 10000000 | tf_op jit(solution)/shard_map/pallas_call | solution.py:516
  56.2 1.6 %copy.8 = bf16[1,512,224]{1,2,0:T(8,128)(2,1)} copy(bf16[1,512,224]{1,2,0:T(8,128)(2,1)} %bitcast.11) | data formatting | bytes 458752
  57.9 1.6 %copy.9 = bf16[256,224]{0,1:T(8,128)(2,1)} copy(bf16[256,224]{0,1:T(8,128)(2,1)} %bitcast.12) | data formatting | bytes 229376

commit v3 on v2

--- a/solution.py
+++ b/solution.py
@@ -345,19 +345,19 @@
     @when(first)
     def _():
         p1_start(x1, 0)
+        wait_for(ready0, count(zl < 3) + count(has_perm, perm_z > zl) + ups_above)
+
+        @when(has_perm)
+        def _():
+            perm_copy().start()
+
+        @when(y == dp)
+        def _():
+            perm_local().start()
+
+        up_start()
         p1_wait(x1, 0)
         ring_first(x1, 0)
-        wait_for(ready0, count(zl < 3) + count(has_perm, perm_z > zl) + ups_above)
-
-        @when(has_perm)
-        def _():
-            perm_copy().start()
-
-        @when(y == dp)
-        def _():
-            perm_local().start()
-
-        up_start()
         ring_second(x1, 0)
 
         @when(has_perm)
@@ -371,6 +371,10 @@
         up_wait()
         p1_start(x2, 1)
         p1_start(x3, 2)
+        p1_wait(x2, 1)
+        ring_first(x2, 1)
+        p1_wait(x3, 2)
+        ring_first(x3, 2)
         ring_rest(x1, 0)
         pltpu.make_async_copy(slot_w, wf, load_sem.at[1]).wait()
         pltpu.make_async_copy(up_w, wd, load_sem.at[2]).wait()
@@ -397,10 +401,6 @@
         z_step(1)
         z_sib(0, 1).start()
         z_sib(0, 0).start()
-        p1_wait(x2, 1)
-        ring_first(x2, 1)
-        p1_wait(x3, 2)
-        ring_first(x3, 2)
         z_step(2)
         ring_second(x2, 1)
         ring_second(x3, 2)

time: 59.6 us -> 55.5 us (0.931)
  the two profiles are of different devices: /device:TPU:17 before, /device:TPU:1 now
where the time goes in v3:
time: 55.5 us; the launch traced here: 55.3 us
  Pallas kernels  51.4 us (93%)
  local copies, waits for them, and re-layouts  3.19 us (6%)
  between operations  0.64 us (1%)
    pallas_call x1, Pallas kernels, local(): pl.pallas_call(kernel, out_shape=(jax.ShapeDtypeStruct((224, 512), BF), j...  51.4 us
    unnamed x2, local copies, waits for them, and re-layouts  3.19 us

profile of v3, /device:TPU:1, one launch (start us, length us, event | category | flops | bytes accessed | tf_op | source)
XLA Modules:
  0.0 55.3 jit_solution(4238400017651675849)
XLA Ops:
  0.6 51.4 %shard_map.59 = (bf16[224,512]{1,0:T(8,128)(2,1)}, bf16[224,256]{1,0:T(8,128)(2,1)}) custom-call(bf16[64,128]{1,0:T(8,128)(2,1)} %bitcast.13, bf16[224,4096]{1,0:T(8,128)(2,1)} %bitcast.9, bf16[224,4096]{1,0:T(8,128)(2,1)} %bitcast.10, bf16[128,4096]{1,0:T(8,128)(2,1)} %cot.1), custom_call_target="tpu_custom_call" | custom-call | flops 1000000000 | bytes 10000000 | tf_op jit(solution)/shard_map/pallas_call | solution.py:516
  52.1 1.6 %copy.8 = bf16[1,512,224]{1,2,0:T(8,128)(2,1)} copy(bf16[1,512,224]{1,2,0:T(8,128)(2,1)} %bitcast.11) | data formatting | bytes 458752
  53.7 1.6 %copy.9 = bf16[256,224]{0,1:T(8,128)(2,1)} copy(bf16[256,224]{0,1:T(8,128)(2,1)} %bitcast.12) | data formatting | bytes 229376

commit v4 on v3

--- a/solution.py
+++ b/solution.py
@@ -439,36 +439,41 @@
             z_step(d)
 
     ring_rest(x2, 1)
-    ring_rest(x3, 2)
     side = jnp.where(first, 0, 2)
     for q in range(4):
         for c in (1, side):
             unit = units.at[q * 2 + 1 - core, c]
             remote(unit, unit, sib_send.at[q, c], sib_recv.at[q, c], sib).wait_recv()
 
+    by_group = both(first, even)
     total_slot = jnp.zeros((224, 512), F32)
+    for pair in range(4):
+        groups = (2 * pair, 2 * pair + 1)
+        rows = [
+            jnp.concatenate(
+                [x2[jnp.where(by_group, g, j), jnp.where(by_group, j, g)] for j in range(8)], axis=0)
+            for g in groups
+        ]
+        total_slot += lax.dot_general(
+            jnp.concatenate([units[g, side] for g in groups], axis=1),
+            jnp.concatenate(rows, axis=1), NT, preferred_element_type=F32)
+    res_slot[...] = total_slot.astype(BF)
+    st_slot = pltpu.make_async_copy(res_slot, out_slot, load_sem.at[0])
+    st_slot.start()
+
+    ring_rest(x3, 2)
     total_up = jnp.zeros((224, 256), F32)
-    by_group = both(first, even)
     for pair in range(4):
-        lefts, ups, rows_slot, rows_up = [], [], [], []
-        for g in (2 * pair, 2 * pair + 1):
-            lefts.append(units[g, side])
-            ups.append(units[g, 1])
-            rows_slot.append(jnp.concatenate(
-                [x2[jnp.where(by_group, g, j), jnp.where(by_group, j, g)] for j in range(8)], axis=0))
+        groups = (2 * pair, 2 * pair + 1)
+        rows = []
+        for g in groups:
             places = [slot_at(core, g, xx) for xx in range(8)]
-            rows_up.append(jnp.concatenate([x3[a, b] for a, b in places], axis=0))
-        total_slot += lax.dot_general(
-            jnp.concatenate(lefts, axis=1), jnp.concatenate(rows_slot, axis=1), NT,
-            preferred_element_type=F32)
+            rows.append(jnp.concatenate([x3[a, b] for a, b in places], axis=0))
         total_up += lax.dot_general(
-            jnp.concatenate(ups, axis=1), jnp.concatenate(rows_up, axis=1), NT,
-            preferred_element_type=F32)
-    res_slot[...] = total_slot.astype(BF)
+            jnp.concatenate([units[g, 1] for g in groups], axis=1),
+            jnp.concatenate(rows, axis=1), NT, preferred_element_type=F32)
     res_up[...] = total_up.astype(BF)
-    st_slot = pltpu.make_async_copy(res_slot, out_slot, load_sem.at[0])
     st_up = pltpu.make_async_copy(res_up, out_up, load_sem.at[1])
-    st_slot.start()
     st_up.start()
 
     @when(first)

time: 55.5 us -> 55.8 us (level)
  no operation moved by 1% of the time
where the time goes in v4:
time: 55.8 us; the launch traced here: 55.6 us
  Pallas kernels  51.7 us (93%)
  local copies, waits for them, and re-layouts  3.19 us (6%)
  between operations  0.64 us (1%)
    pallas_call x1, Pallas kernels, local(): pl.pallas_call(kernel, out_shape=(jax.ShapeDtypeStruct((224, 512), BF), j...  51.7 us
    unnamed x2, local copies, waits for them, and re-layouts  3.19 us

profile of v4, /device:TPU:1, one launch (start us, length us, event | category | flops | bytes accessed | tf_op | source)
XLA Modules:
  0.0 55.6 jit_solution(10084521262303315584)
XLA Ops:
  0.6 51.7 %shard_map.59 = (bf16[224,512]{1,0:T(8,128)(2,1)}, bf16[224,256]{1,0:T(8,128)(2,1)}) custom-call(bf16[64,128]{1,0:T(8,128)(2,1)} %bitcast.13, bf16[224,4096]{1,0:T(8,128)(2,1)} %bitcast.9, bf16[224,4096]{1,0:T(8,128)(2,1)} %bitcast.10, bf16[128,4096]{1,0:T(8,128)(2,1)} %cot.1), custom_call_target="tpu_custom_call" | custom-call | flops 1000000000 | bytes 10000000 | tf_op jit(solution)/shard_map/pallas_call | solution.py:521
  52.4 1.6 %copy.8 = bf16[1,512,224]{1,2,0:T(8,128)(2,1)} copy(bf16[1,512,224]{1,2,0:T(8,128)(2,1)} %bitcast.11) | data formatting | bytes 458752
  54.0 1.6 %copy.9 = bf16[256,224]{0,1:T(8,128)(2,1)} copy(bf16[256,224]{0,1:T(8,128)(2,1)} %bitcast.12) | data formatting | bytes 229376
